TPU v7x, 128 devices: a whole 4x4x4 slice. The times are simulated.
128 devices in a mesh: row: 16 (over x_lo, z, core), col: 8 (over x_hi, y).
Axes of the slice: x: 4 (x_hi: 2, x_lo: 2; x = x_hi * 2 + x_lo), y: 4, z: 4, core: 2. Of those that a mesh axis runs over, the one named last changes fastest.
Arguments:
- alignment_features: bfloat16 [512, 1024, 256], P('row', 'col'), may hold values from -6 to 6
- standardize_scale: float32 [256], replicated, may hold values from 0.5 to 1.5
- source_matrix: bfloat16 [256, 32], replicated, may hold values from -0.375 to 0.375
- target_matrix: bfloat16 [256, 32], replicated, may hold values from -0.375 to 0.375
- final_matrix: bfloat16 [1024, 128], replicated, may hold values from -3 to 3
- final_offset: float32 [128], replicated, may hold values from -4 to 4
Outputs:
- pair_update: bfloat16 [1024, 1024, 128], P('row', 'col')
All inputs are finite; a program needn't handle non-finite values.
Results may differ from a plain program's by a relative error of at most 0.0054.
Values may be sent and summed in bfloat16 or wider, within the bound.
A program may use at most 64 MiB of HBM per device.

v0:
```python
import jax
import jax.numpy as jnp
from jax import lax
from jax.sharding import PartitionSpec as P

HALF_WIDTH = 32
OUTC = 128
BLK = 16


def body(
    alignment_features, standardize_scale, source_matrix, target_matrix, final_matrix, final_offset
):
    element_number = alignment_features.astype(jnp.float32)
    center = jnp.mean(element_number, axis=-1, keepdims=True)
    spread = jnp.mean(jnp.square(element_number - center), axis=-1, keepdims=True)
    standardized = (
        (element_number - center) * lax.rsqrt(spread + 1e-05) * standardize_scale
    ).astype(jnp.bfloat16)
    seq_local, col_res, channels = standardized.shape
    unrolled_matrix = standardized.reshape(seq_local * col_res, channels)
    left_local = (
        jnp.dot(unrolled_matrix, source_matrix, preferred_element_type=jnp.float32)
        .astype(jnp.bfloat16)
        .reshape(seq_local, col_res, HALF_WIDTH)
    )
    right_local = (
        jnp.dot(unrolled_matrix, target_matrix, preferred_element_type=jnp.float32)
        .astype(jnp.bfloat16)
        .reshape(seq_local, col_res, HALF_WIDTH)
    )
    ratio = lax.axis_size("row") // lax.axis_size("col")
    row_res = col_res // ratio
    right_full = lax.all_gather(right_local, "row", axis=0, tiled=True)
    left_wide = lax.all_gather(left_local, "col", axis=1, tiled=True)
    left_full = lax.all_to_all(left_wide, "row", split_axis=1, concat_axis=0, tiled=True)
    seq_total = right_full.shape[0]
    weight_out = final_matrix.reshape(HALF_WIDTH, HALF_WIDTH, OUTC)
    blocks = jnp.moveaxis(left_full.reshape(seq_total, row_res // BLK, BLK, HALF_WIDTH), 1, 0)

    def one_block(block):
        outer = (
            jnp.einsum("sia,sjb->ijab", block, right_full, preferred_element_type=jnp.float32)
            / seq_total
        )
        outer = outer.astype(jnp.bfloat16)
        result = (
            jnp.einsum("ijab,abe->ije", outer, weight_out, preferred_element_type=jnp.float32)
            + final_offset
        )
        return result.astype(jnp.bfloat16)

    return lax.map(one_block, blocks).reshape(row_res, col_res, OUTC)


def solution(mesh):
    in_specs = (P("row", "col", None), P(), P(), P(), P(), P())
    out_specs = P("row", "col", None)
    return jax.shard_map(body, mesh=mesh, in_specs=in_specs, out_specs=out_specs, check_vma=False)
```

profile of v0, /device:TPU:0, one launch (start us, length us, event | category | flops | bytes accessed | tf_op | source)
XLA Modules:
  0.0 196.9 jit_solution(7486183342941758936)
XLA Ops:
  6.5 0.0 copy-start
  6.5 0.0 all-gather.3.cloned.1.call-start
  6.5 2.4 %convert_reduce_fusion = f32[32,128]{1,0:T(8,128)S(1)} fusion(bf16[32,128,256]{2,1,0:T(8,128)(2,1)} %param.8), kind=kLoop, calls=%fused_computation.17 | loop fusion | flops 2093056 | bytes 2113536 | tf_op jit(solution)/shard_map/reduce_sum | solution.py:15
  8.9 0.0 copy-done.1
  8.9 1.3 fusion.45
  10.3 0.0 copy-done.5
  10.3 1.4 fusion.47
  11.7 0.0 copy-start.2
  11.7 0.0 copy-start.4
  11.7 1.3 copy-done.2
  13.0 0.7 fusion.48
  13.7 0.8 copy.32
  14.5 0.0 all-gather.3.cloned.1.call-update
  14.5 0.0 all-gather.5.cloned.1.call-start
  14.6 2.3 %fusion.49 = bf16[4,8,32,128]{3,1,2,0:T(8,128)(2,1)S(1)} fusion(bf16[4096,256]{1,0:T(8,128)(2,1)} %bitcast.98, bf16[256,32]{0,1:T(8,128)(2,1)S(1)} %copy-done.4), kind=kOutput, calls=%fused_computation.26 | convolution fusion | flops 67239936 | bytes 2375680 | tf_op jit(solution)/shard_map/dot_general | solution.py:28
  16.9 0.7 copy.30
  17.6 0.0 all-gather.5.cloned.1.call-update
  17.7 53.8 %all-gather.3.cloned.1.call-done = bf16[32,1024,32]{1,2,0:T(8,128)(2,1)} async-done(((bf16[32,128,32]{1,2,0:T(8,128)(2,1)}), bf16[32,1024,32]{1,2,0:T(8,128)(2,1)}) %all-gather.3.cloned.1.call-update) | async-done | bytes 2097168 | tf_op jit(solution)/shard_map/all_gather | solution.py:35
  71.5 12.5 %copy.21 = bf16[32,1024,32]{2,0,1:T(8,128)(2,1)} copy(bf16[32,1024,32]{1,2,0:T(8,128)(2,1)} %all-gather.3.cloned.1.call-done) | data formatting | bytes 4194304 | tf_op jit(solution)/shard_map/all_gather | solution.py:35
  84.0 14.6 %reshape.43 = bf16[16,2,32768]{2,1,0:T(2,128)(2,1)} reshape(bf16[1024,32,32]{2,1,0:T(8,128)(2,1)} %bitcast.95) | data formatting | bytes 4194304
  98.5 4.7 %all-to-all-start = ((bf16[16,2,32768]{2,1,0:T(2,128)(2,1)}), bf16[16,2,32768]{2,1,0:T(2,128)(2,1)S(1)}, u32[]{:S(2)}, u32[]{:S(2)}) async-start(bf16[16,2,32768]{2,1,0:T(2,128)(2,1)} %reshape.43), calls=%async_computation | async-start | bytes 4194304 | tf_op jit(solution)/shard_map/all_to_all | solution.py:36
  103.3 0.1 copy.24
  103.4 28.6 %all-to-all-done = bf16[16,2,32768]{2,1,0:T(2,128)(2,1)S(1)} async-done(((bf16[16,2,32768]{2,1,0:T(2,128)(2,1)}), bf16[16,2,32768]{2,1,0:T(2,128)(2,1)S(1)}, u32[]{:S(2)}, u32[]{:S(2)}) %all-to-all-start) | async-done | bytes 2097184 | tf_op jit(solution)/shard_map/all_to_all | solution.py:36
  132.0 8.9 %reshape.44 = bf16[1024,32,32]{2,1,0:T(8,128)(2,1)} reshape(bf16[16,2,32768]{2,1,0:T(2,128)(2,1)S(1)} %all-to-all-done) | data formatting | bytes 4194304
  140.8 12.5 %copy.23 = bf16[16,32,64,32]{1,0,3,2:T(8,128)(2,1)} copy(bf16[16,32,64,32]{3,1,2,0:T(8,128)(2,1)} %bitcast.96) | data formatting | bytes 4194304 | tf_op jit(solution)/shard_map/all_to_all | solution.py:36
  153.4 10.9 %reshape.35 = bf16[512,4,16,32]{0,3,2,1:T(8,128)(2,1)S(1)} reshape(bf16[16,32,64,32]{1,0,3,2:T(8,128)(2,1)} %copy.23) | data formatting | bytes 4194304 | tf_op jit(solution)/shard_map/reshape | solution.py:39
  164.3 0.0 all-gather.5.cloned.1.call-done
  164.4 25.7 %while.10 = (s32[]{:T(128)}, bf16[4,16,128,128]{3,2,1,0:T(8,128)(2,1)}, bf16[4,512,16,32]{1,3,2,0:T(8,128)(2,1)S(1)}, bf16[512,128,32]{1,0,2:T(8,128)(2,1)}, bf1...) while((s32[]{:T(128)}, bf16[4,16,128,128]{3,2,1,0:T(8,128)(2,1)}, ...), condition=%wide.region_3.4_spmd, body=%wide.region_2.3_spmd.sunk | while | flops 2689073152 | bytes 5506637 | solution.py:53
  164.4 6.4 %fusion.63 = bf16[4,16,128,128]{3,2,1,0:T(8,128)(2,1)} fusion(bf16[4,16,128,128]{3,2,1,0:T(8,128)(2,1)} %get-tuple-element.113, s32[]{:T(128)} %get-tuple-element.112, bf16[512,128,32]{1,0,2:T(8,128)(2,1)} %get-tuple-element.122, f32[128]{0:T(128)S(1)} %get-tuple-element.124, bf16[4,512,16,32]{1,3,2,0:T(8,128)(2,1)S(1)} %get-tuple-element.121, ...), kind=kOutput, calls=%fused_computation.10.clone.1 | convolution fusion | flops 2689073152 | bytes 5506560 | tf_op jit(solution)/shard_map/while/body/eval_jaxpr/ijab,abe->ije/dot_general | solution.py:48
  170.8 6.4 %fusion.63 = bf16[4,16,128,128]{3,2,1,0:T(8,128)(2,1)} fusion(bf16[4,16,128,128]{3,2,1,0:T(8,128)(2,1)} %get-tuple-element.113, s32[]{:T(128)} %get-tuple-element.112, bf16[512,128,32]{1,0,2:T(8,128)(2,1)} %get-tuple-element.122, f32[128]{0:T(128)S(1)} %get-tuple-element.124, bf16[4,512,16,32]{1,3,2,0:T(8,128)(2,1)S(1)} %get-tuple-element.121, ...), kind=kOutput, calls=%fused_computation.10.clone.1 | convolution fusion | flops 2689073152 | bytes 5506560 | tf_op jit(solution)/shard_map/while/body/eval_jaxpr/ijab,abe->ije/dot_general | solution.py:48
  177.2 6.4 %fusion.63 = bf16[4,16,128,128]{3,2,1,0:T(8,128)(2,1)} fusion(bf16[4,16,128,128]{3,2,1,0:T(8,128)(2,1)} %get-tuple-element.113, s32[]{:T(128)} %get-tuple-element.112, bf16[512,128,32]{1,0,2:T(8,128)(2,1)} %get-tuple-element.122, f32[128]{0:T(128)S(1)} %get-tuple-element.124, bf16[4,512,16,32]{1,3,2,0:T(8,128)(2,1)S(1)} %get-tuple-element.121, ...), kind=kOutput, calls=%fused_computation.10.clone.1 | convolution fusion | flops 2689073152 | bytes 5506560 | tf_op jit(solution)/shard_map/while/body/eval_jaxpr/ijab,abe->ije/dot_general | solution.py:48
  183.7 6.4 %fusion.63 = bf16[4,16,128,128]{3,2,1,0:T(8,128)(2,1)} fusion(bf16[4,16,128,128]{3,2,1,0:T(8,128)(2,1)} %get-tuple-element.113, s32[]{:T(128)} %get-tuple-element.112, bf16[512,128,32]{1,0,2:T(8,128)(2,1)} %get-tuple-element.122, f32[128]{0:T(128)S(1)} %get-tuple-element.124, bf16[4,512,16,32]{1,3,2,0:T(8,128)(2,1)S(1)} %get-tuple-element.121, ...), kind=kOutput, calls=%fused_computation.10.clone.1 | convolution fusion | flops 2689073152 | bytes 5506560 | tf_op jit(solution)/shard_map/while/body/eval_jaxpr/ijab,abe->ije/dot_general | solution.py:48
  (11 shorter events, 0.0 us)
Async XLA Ops:
  6.5 6.5 %copy-start = (bf16[256,32]{0,1:T(8,128)(2,1)S(1)}, bf16[256,32]{0,1:T(8,128)(2,1)}, u32[]{:S(2)}) copy-start(bf16[256,32]{0,1:T(8,128)(2,1)} %param.10) | copy-start | bytes 49156
  6.5 2.4 %copy-start.1 = (bf16[32,128,256]{2,1,0:T(8,128)(2,1)S(1)}, bf16[32,128,256]{2,1,0:T(8,128)(2,1)}, u32[]{:S(2)}) copy-start(bf16[32,128,256]{2,1,0:T(8,128)(2,1)} %param.8) | copy-start | bytes 6291460
  6.5 3.7 %copy-start.5 = (f32[256]{0:T(256)S(1)}, f32[256]{0:T(256)}, u32[]{:S(2)}) copy-start(f32[256]{0:T(256)} %param.9) | copy-start | bytes 3076
  6.5 64.9 %all-gather.3.cloned.1.call-start = ((), (), s32[]{:S(2)}) async-start(), calls=%async_computation.1 | async-start | bytes 2359296 | tf_op jit(solution)/shard_map/all_gather | solution.py:35
  11.7 1.3 copy-start.2
  11.7 2.9 %copy-start.4 = (bf16[256,32]{0,1:T(8,128)(2,1)S(1)}, bf16[256,32]{0,1:T(8,128)(2,1)}, u32[]{:S(2)}) copy-start(bf16[256,32]{0,1:T(8,128)(2,1)} %param.11) | copy-start | bytes 49156
  14.5 149.8 %all-gather.5.cloned.1.call-start = ((), (), s32[]{:S(2)}) async-start(), calls=%async_computation.2 | async-start | bytes 4456448 | tf_op jit(solution)/shard_map/all_gather | solution.py:34
  98.5 4.7 %copy-start.3 = (bf16[1024,128]{1,0:T(8,128)(2,1)S(1)}, bf16[1024,128]{1,0:T(8,128)(2,1)}, u32[]{:S(2)}) copy-start(bf16[1024,128]{1,0:T(8,128)(2,1)} %param.12) | copy-start | bytes 786436
  98.5 33.5 %all-to-all-start = ((bf16[16,2,32768]{2,1,0:T(2,128)(2,1)}), bf16[16,2,32768]{2,1,0:T(2,128)(2,1)S(1)}, u32[]{:S(2)}, u32[]{:S(2)}) async-start(bf16[16,2,32768]{2,1,0:T(2,128)(2,1)} %reshape.43), calls=%async_computation | async-start | bytes 4194304 | tf_op jit(solution)/shard_map/all_to_all | solution.py:36
  153.4 11.0 %copy-start.6 = (f32[128]{0:T(128)S(1)}, f32[128]{0:T(128)}, u32[]{:S(2)}) copy-start(f32[128]{0:T(128)} %param.13) | copy-start | bytes 1540
Sparse Core Ops, SparseCore 0:
  14.7 56.7 all-gather.2
  73.1 36.5 all-gather.4
where the time goes:
time: 200 us; the launch traced here: 197 us
  waiting for transfers between devices  82.5 us (41%)
  local copies, waits for them, and re-layouts  62.3 us (31%)
  matrix products  28.7 us (14%)
  between operations  13.5 us (7%)
  other arithmetic  5.1 us (3%)
  starting transfers between devices  4.73 us (2%)
    all_gather x1, waiting for transfers between devices, body(): left_wide = lax.all_gather(left_local, 'col', axis=1, tiled=True)  53.8 us
    all_to_all x1, waiting for transfers between devices, body(): lax.all_to_all(left_wide, 'row', split_axis=1, concat_axis=0, tiled=True)  28.6 us
    dot_general x4, matrix products, one_block(): jnp.einsum('ijab,abe->ije', outer, weight_out, preferred_element_type=jnp...  25.7 us
    unnamed x17, local copies, waits for them, and re-layouts  25.5 us
    all_to_all x1, local copies, waits for them, and re-layouts, body(): lax.all_to_all(left_wide, 'row', split_axis=1, concat_axis=0, tiled=True)  12.5 us
    all_gather x1, local copies, waits for them, and re-layouts, body(): left_wide = lax.all_gather(left_local, 'col', axis=1, tiled=True)  12.5 us
    reshape x1, local copies, waits for them, and re-layouts, body(): left_full.reshape(seq_total, row_res // BLK, BLK, HALF_WIDTH)  10.9 us
    all_to_all x1, starting transfers between devices, body(): lax.all_to_all(left_wide, 'row', split_axis=1, concat_axis=0, tiled=True)  4.68 us
  transfers between devices with their start and end apart: 3, of which 2 were waited for; matrix products, arithmetic and copies ran while one was open for 32% of the time, Pallas kernels for 0%

commit v1 on v0

v1 whole, which is shorter than its diff:
```python
import jax
import jax.numpy as jnp
from jax import lax
from jax.experimental import pallas as pl
from jax.experimental.pallas import tpu as pltpu
from jax.sharding import PartitionSpec as P

MESH = pl.DeviceIdType.MESH
BF16, F32 = jnp.bfloat16, jnp.float32
SEQ, RES, CH = 32, 128, 256
HALF, OUTC = 32, 128
ROWS, COLS = 16, 8
SEQ_ALL = SEQ * ROWS
OCT = 8
PIECE = OCT * HALF
NQ = 4
QL = HALF * RES // NQ
NT = (((1,), (1,)), ((), ()))

R_ROLES = ("sib", "xp", "dn", "up", "oa", "ob", "xdn", "xup", "xoa", "xob")
L_ROLES = ("xp", "dn", "up", "oa", "ob", "xdn", "xup", "xoa", "xob")


def project(x_ref, scale_ref, wl_ref, wr_ref, z_ref):
    wt = jnp.concatenate([wl_ref[...], wr_ref[...]], axis=1).astype(F32).T * scale_ref[...]
    hi = wt.astype(BF16)
    lo = (wt - hi.astype(F32)).astype(BF16)
    colsum = jnp.sum(hi.astype(F32) + lo.astype(F32), axis=1, keepdims=True)
    ones = jnp.ones((16, CH), BF16)
    lhs = jnp.concatenate([hi, lo, ones], axis=0)
    step = 8

    def chunk(k, carry):
        xc = x_ref[pl.ds(k * step, step)].reshape(step * RES, CH)
        p = lax.dot_general(lhs, xc, NT, preferred_element_type=F32)
        xf = xc.astype(F32)
        sq = xf * xf
        sqh = sq.astype(BF16)
        sql = (sq - sqh.astype(F32)).astype(BF16)
        s2 = lax.dot_general(ones, sqh, NT, preferred_element_type=F32) + lax.dot_general(
            ones, sql, NT, preferred_element_type=F32
        )
        mean = p[128:136] * (1.0 / CH)
        mh = mean.astype(BF16).astype(F32)
        ml = mean - mh
        var = (s2[0:8] * (1.0 / CH) - mh * mh) - ml * (2.0 * mh + ml)
        rstd = lax.rsqrt(jnp.maximum(var, 0.0) + 1e-05)
        y = (p[0:64] + p[64:128] - colsum * mean[0:1]) * rstd[0:1]
        for s in range(step):
            z_ref[k * step + s] = y[:, s * RES : (s + 1) * RES]
        return carry

    lax.fori_loop(0, SEQ // step, chunk, 0)


def kernel(
    x_ref, scale_ref, wl_ref, wr_ref, w_ref, off_ref, out_ref,
    z_ref, zl_ref, yl_ref, lsend, lt, lf, rf, w2t, wf, outv,
    t_ss, t_rs, l_ss, l_rs, r_ss, r_rs, f_ss, f_rs, o_s,
):
    r, c = lax.axis_index("row"), lax.axis_index("col")
    xl, z, h = r // 8, (r // 2) % 4, r % 2
    xh, y = c // 4, c % 4

    def row_of(xl_, z_, h_):
        return xl_ * 8 + lax.rem(z_ + 4, 4) * 2 + h_

    def col_of(xh_, y_):
        return xh_ * 4 + lax.rem(y_ + 4, 4)

    sib = (row_of(xl, z, 1 - h), c)
    r_dev = {"xp": (row_of(1 - xl, z, h), c), "up": (row_of(xl, z + 1, h), c), "dn": (row_of(xl, z - 1, h), c)}
    l_dev = {"xp": (r, col_of(1 - xh, y)), "up": (r, col_of(xh, y + 1)), "dn": (r, col_of(xh, y - 1))}

    barrier = pltpu.get_barrier_semaphore()
    owner = r // 2
    for dev in (sib, *r_dev.values(), *l_dev.values()):
        pl.semaphore_signal(barrier, inc=1, device_id=dev, device_id_type=MESH)
    for k in range(ROWS):

        @pl.when(jnp.logical_or(k != r, owner != c))
        def _():
            pl.semaphore_signal(barrier, inc=1, device_id=(k, owner), device_id_type=MESH)

    project(x_ref, scale_ref, wl_ref, wr_ref, z_ref)

    for a in range(HALF):
        yl_ref[a] = z_ref[:, a, :].astype(BF16)
    eye = (
        lax.broadcasted_iota(jnp.int32, (RES, RES), 0) == lax.broadcasted_iota(jnp.int32, (RES, RES), 1)
    ).astype(BF16)
    for t in range(8):
        b = jnp.concatenate([yl_ref[t + 8 * g] for g in range(4)], axis=0)
        zl_ref[:, t, :] = lax.dot_general(eye, b, NT, preferred_element_type=F32)
    lsend[...] = zl_ref[...].reshape(RES * 8, 128).astype(BF16)

    pl.semaphore_wait(barrier, jnp.where(owner == c, 22, 23))

    for k in range(ROWS):
        o = lax.rem(r + k, ROWS)
        to_row, to_col = 2 * c + o // COLS, lax.rem(o, COLS)
        src = lsend.at[pl.ds(pl.multiple_of(o * 64, 64), 64)]
        mine = jnp.logical_and(to_row == r, to_col == c)

        @pl.when(mine)
        def _():
            pltpu.make_async_copy(src, lt.at[r], t_rs.at[r]).start()

        @pl.when(jnp.logical_not(mine))
        def _():
            pltpu.make_async_remote_copy(
                src, lt.at[r], t_ss.at[k], t_rs.at[r], device_id=(to_row, to_col), device_id_type=MESH
            ).start()

    for b in range(HALF):
        rf[pl.ds(pl.multiple_of(r * SEQ, SEQ), SEQ), pl.ds(b * RES, RES)] = z_ref[:, HALF + b, :].astype(BF16)

    def r_ref(q, xl_, z_, h_, half=None):
        rows = row_of(xl_, z_, h_) * SEQ
        n = SEQ
        if half is not None:
            rows, n = rows + half * (SEQ // 2), SEQ // 2
        return rf.at[pl.ds(pl.multiple_of(rows, n), n), pl.ds(q * QL, QL)]

    def r_block(q, role, h_):
        return {
            "own": lambda: r_ref(q, xl, z, h_),
            "xp": lambda: r_ref(q, 1 - xl, z, h_),
            "dn": lambda: r_ref(q, xl, z - 1, h_),
            "up": lambda: r_ref(q, xl, z + 1, h_),
            "oa": lambda: r_ref(q, xl, z + 2, h_, 0),
            "ob": lambda: r_ref(q, xl, z + 2, h_, 1),
            "xdn": lambda: r_ref(q, 1 - xl, z - 1, h_),
            "xup": lambda: r_ref(q, 1 - xl, z + 1, h_),
            "xoa": lambda: r_ref(q, 1 - xl, z + 2, h_, 0),
            "xob": lambda: r_ref(q, 1 - xl, z + 2, h_, 1),
        }[role]()

    def copy(src, sems, at, dev):
        return pltpu.make_async_remote_copy(
            src, src, sems[0].at[at], sems[1].at[at], device_id=dev, device_id_type=MESH
        )

    sends = []

    def r_send(q, role, src, dev):
        d = copy(src, (r_ss, r_rs), (q, R_ROLES.index(role)), dev)
        d.start()
        sends.append(d)

    def f_send(q, role):
        d = copy(r_block(q, role, h), (f_ss, f_rs), (q, R_ROLES.index(role)), sib)
        d.start()
        sends.append(d)

    def r_wait(q, role):
        ref = r_block(q, "own" if role == "sib" else role, 1 - h if role == "sib" else h)
        pltpu.make_async_copy(ref, ref, r_rs.at[q, R_ROLES.index(role)]).wait()

    def f_wait(q, role):
        ref = r_block(q, role, 1 - h)
        pltpu.make_async_copy(ref, ref, f_rs.at[q, R_ROLES.index(role)]).wait()

    def r_stage0(q):
        own = r_ref(q, xl, z, h)
        r_send(q, "xp", own, r_dev["xp"])
        r_send(q, "dn", own, r_dev["up"])
        r_send(q, "up", own, r_dev["dn"])
        r_send(q, "sib", own, sib)

    def r_stage1(q):
        r_wait(q, "dn")
        r_send(q, "oa", r_ref(q, xl, z - 1, h, 0), r_dev["up"])
        r_wait(q, "up")
        r_send(q, "ob", r_ref(q, xl, z + 1, h, 1), r_dev["dn"])
        r_wait(q, "xp")
        xp = r_block(q, "xp", h)
        r_send(q, "xdn", xp, r_dev["up"])
        r_send(q, "xup", xp, r_dev["dn"])
        for role in ("dn", "up", "xp"):
            f_send(q, role)

    def r_stage2(q):
        r_wait(q, "xdn")
        r_send(q, "xoa", r_ref(q, 1 - xl, z - 1, h, 0), r_dev["up"])
        r_wait(q, "xup")
        r_send(q, "xob", r_ref(q, 1 - xl, z + 1, h, 1), r_dev["dn"])
        for role in ("xdn", "xup"):
            f_send(q, role)
        for role in ("oa", "ob"):
            r_wait(q, role)
            f_send(q, role)

    def r_stage3(q):
        for role in ("xoa", "xob"):
            r_wait(q, role)
            f_send(q, role)

    def r_stage4(q):
        r_wait(q, "sib")
        for role in R_ROLES[1:]:
            f_wait(q, role)

    def l_ref(xh_, y_, half=None):
        rows, n = col_of(xh_, y_) * PIECE, PIECE
        if half is not None:
            rows, n = rows + half * (PIECE // 2), PIECE // 2
        return lf.at[pl.ds(pl.multiple_of(rows, n), n)]

    def l_block(role):
        return {
            "xp": lambda: l_ref(1 - xh, y),
            "dn": lambda: l_ref(xh, y - 1),
            "up": lambda: l_ref(xh, y + 1),
            "oa": lambda: l_ref(xh, y + 2, 0),
            "ob": lambda: l_ref(xh, y + 2, 1),
            "xdn": lambda: l_ref(1 - xh, y - 1),
            "xup": lambda: l_ref(1 - xh, y + 1),
            "xoa": lambda: l_ref(1 - xh, y + 2, 0),
            "xob": lambda: l_ref(1 - xh, y + 2, 1),
        }[role]()

    def l_send(role, src, dev):
        d = copy(src, (l_ss, l_rs), (L_ROLES.index(role),), dev)
        d.start()
        sends.append(d)

    def l_wait(role):
        ref = l_block(role)
        pltpu.make_async_copy(ref, ref, l_rs.at[L_ROLES.index(role)]).wait()

    def l_stage0():
        for k in range(ROWS):
            pltpu.make_async_copy(lt.at[k], lt.at[k], t_rs.at[k]).wait()
        i0 = lax.broadcasted_iota(jnp.int32, (512, 512), 0)
        i1 = lax.broadcasted_iota(jnp.int32, (512, 512), 1)
        to = ((i0 // 32) % 4) * 128 + (i0 // 128) * 32 + i0 % 32
        perm = (to == i1).astype(BF16)
        for g in range(4):
            v = jnp.concatenate([lt[4 * g + k] for k in range(4)], axis=1)
            w = jnp.dot(v, perm, preferred_element_type=F32)
            w = jnp.concatenate([w[:, 128 * k : 128 * (k + 1)].reshape(OCT, 8, 128) for k in range(4)], axis=1)
            lf[pl.ds(pl.multiple_of(c * PIECE, PIECE), PIECE), pl.ds(g * 128, 128)] = w.reshape(PIECE, 128).astype(BF16)
        own = l_ref(xh, y)
        l_send("xp", own, l_dev["xp"])
        l_send("dn", own, l_dev["up"])
        l_send("up", own, l_dev["dn"])

    def l_stage1():
        l_wait("dn")
        l_send("oa", l_ref(xh, y - 1, 0), l_dev["up"])
        l_wait("up")
        l_send("ob", l_ref(xh, y + 1, 1), l_dev["dn"])
        l_wait("xp")
        xp = l_ref(1 - xh, y)
        l_send("xdn", xp, l_dev["up"])
        l_send("xup", xp, l_dev["dn"])

    def l_stage2():
        l_wait("xdn")
        l_send("xoa", l_ref(1 - xh, y - 1, 0), l_dev["up"])
        l_wait("xup")
        l_send("xob", l_ref(1 - xh, y + 1, 1), l_dev["dn"])

    def l_stage3():
        for role in ("oa", "ob", "xoa", "xob"):
            l_wait(role)

    for q in range(NQ):
        r_stage0(q)
    l_stage0()

    wf[...] = w_ref[...].astype(F32).reshape(HALF, HALF, OUTC)
    for b in range(HALF):
        w2t[:, pl.ds(b * HALF, HALF)] = wf[:, b, :].T.astype(BF16)

    r_stage1(0)
    r_stage1(1)
    l_stage1()
    r_stage2(0)
    r_stage1(2)
    r_stage2(1)
    r_stage3(0)
    r_stage1(3)
    r_stage2(2)
    r_stage3(1)
    l_stage2()
    r_stage2(3)
    r_stage3(2)
    r_stage3(3)
    for q in range(NQ):
        r_stage4(q)
    l_stage3()

    off = off_ref[...]

    def piece(m, carry):
        lhs = lf[pl.ds(pl.multiple_of(m * PIECE, PIECE), PIECE)]
        acc = jnp.zeros((OUTC, OCT * RES), F32)
        for q in range(NQ):
            o = jnp.dot(lhs, rf[:, q * QL : (q + 1) * QL], preferred_element_type=F32).astype(BF16)
            rhs = jnp.concatenate(
                [
                    jnp.concatenate([o[i * HALF : (i + 1) * HALF, b * RES : (b + 1) * RES] for b in range(8)], axis=0)
                    for i in range(OCT)
                ],
                axis=1,
            )
            acc += jnp.dot(w2t[:, q * 256 : (q + 1) * 256], rhs, preferred_element_type=F32)
        for i in range(OCT):
            t = acc[:, i * RES : (i + 1) * RES].T
            outv[m * OCT + i] = (t * (1.0 / SEQ_ALL) + off).astype(BF16)
        rows = pl.ds(m * OCT, OCT)
        pltpu.make_async_copy(outv.at[rows], out_ref.at[rows], o_s.at[m]).start()
        return carry

    lax.fori_loop(0, COLS, piece, 0)
    for m in range(COLS):
        rows = pl.ds(m * OCT, OCT)
        pltpu.make_async_copy(outv.at[rows], out_ref.at[rows], o_s.at[m]).wait()
    for k in range(ROWS):
        o = lax.rem(r + k, ROWS)
        mine = jnp.logical_and(2 * c + o // COLS == r, lax.rem(o, COLS) == c)

        @pl.when(jnp.logical_not(mine))
        def _():
            src = lsend.at[pl.ds(pl.multiple_of(o * 64, 64), 64)]
            pltpu.make_async_copy(src, src, t_ss.at[k]).wait()

    for d in sends:
        d.wait_send()


def body(x, scale, wl, wr, w, off):
    dma = pltpu.SemaphoreType.DMA
    vmem = pl.BlockSpec(memory_space=pltpu.VMEM)
    return pl.pallas_call(
        kernel,
        out_shape=jax.ShapeDtypeStruct((64, RES, OUTC), BF16),
        in_specs=[vmem] * 6,
        out_specs=pl.BlockSpec(memory_space=pl.ANY),
        scratch_shapes=[
            pltpu.VMEM((SEQ, 64, RES), F32),
            pltpu.VMEM((RES, 8, 128), F32),
            pltpu.VMEM((HALF, SEQ, RES), BF16),
            pltpu.VMEM((RES * 8, 128), BF16),
            pltpu.VMEM((ROWS, 64, 128), BF16),
            pltpu.VMEM((COLS * PIECE, SEQ_ALL), BF16),
            pltpu.VMEM((SEQ_ALL, HALF * RES), BF16),
            pltpu.VMEM((OUTC, HALF * HALF), BF16),
            pltpu.VMEM((HALF, HALF, OUTC), F32),
            pltpu.VMEM((64, RES, OUTC), BF16),
            dma((ROWS,)), dma((ROWS,)),
            dma((len(L_ROLES),)), dma((len(L_ROLES),)),
            dma((NQ, len(R_ROLES))), dma((NQ, len(R_ROLES))),
            dma((NQ, len(R_ROLES))), dma((NQ, len(R_ROLES))),
            dma((COLS,)),
        ],
        compiler_params=pltpu.CompilerParams(
            collective_id=0, has_side_effects=True, vmem_limit_bytes=48 * 2**20
        ),
        cost_estimate=pl.CostEstimate(flops=11 * 10**9, bytes_accessed=5 * 10**6, transcendentals=4096),
        name="outer_product_mean",
    )(x, scale.reshape(1, CH), wl, wr, w, off.reshape(1, OUTC))


def solution(mesh):
    in_specs = (P("row", "col", None), P(), P(), P(), P(), P())
    return jax.shard_map(body, mesh=mesh, in_specs=in_specs, out_specs=P("row", "col", None), check_vma=False)
```

time: 200 us -> 65.8 us (0.33)
  the two profiles are of different devices: /device:TPU:0 before, /device:TPU:3 now
where the time goes in v1:
time: 65.8 us; the launch traced here: 65.5 us
  Pallas kernels  58.6 us (89%)
  local copies, waits for them, and re-layouts  6.86 us (10%)
    pallas_call x1, Pallas kernels, body(): pl.pallas_call(kernel, out_shape=jax.ShapeDtypeStruct((64, RES, OUTC), BF...  58.6 us
    unnamed x11, local copies, waits for them, and re-layouts  6.86 us

profile of v1, /device:TPU:3, one launch (start us, length us, event | category | flops | bytes accessed | tf_op | source)
XLA Modules:
  0.0 65.5 jit_solution(16063681443533670610)
XLA Ops:
  0.0 0.8 %copy.7.wl_ref = bf16[256,32]{1,0:T(8,128)(2,1)S(1)} copy(bf16[256,32]{0,1:T(8,128)(2,1)} %param.8) | data formatting | bytes 32768 | tf_op args[2]
  0.8 0.8 %copy.8.wr_ref = bf16[256,32]{1,0:T(8,128)(2,1)S(1)} copy(bf16[256,32]{0,1:T(8,128)(2,1)} %param.9) | data formatting | bytes 32768 | tf_op args[3]
  1.7 0.0 copy-start
  1.7 1.6 %copy-done = bf16[32,128,256]{2,1,0:T(8,128)(2,1)S(1)} copy-done((bf16[32,128,256]{2,1,0:T(8,128)(2,1)S(1)}, bf16[32,128,256]{2,1,0:T(8,128)(2,1)}, u32[]{:S(2)}) %copy-start) | copy-done | bytes 2097176
  3.3 0.0 copy-start.1
  3.3 0.9 %copy-done.1 = bf16[1024,128]{1,0:T(8,128)(2,1)S(1)} copy-done((bf16[1024,128]{1,0:T(8,128)(2,1)S(1)}, bf16[1024,128]{1,0:T(8,128)(2,1)}, u32[]{:S(2)}) %copy-start.1) | copy-done | bytes 262168
  4.2 0.0 copy-start.2
  4.2 0.7 %copy-done.2 = f32[256]{0:T(256)S(1)} copy-done((f32[256]{0:T(256)S(1)}, f32[256]{0:T(256)}, u32[]{:S(2)}) %copy-start.2) | copy-done | bytes 1048
  4.9 0.0 copy-start.3
  4.9 0.7 copy-done.3
  5.6 58.6 %outer_product_mean.1 = bf16[64,128,128]{2,1,0:T(8,128)(2,1)S(1)} custom-call(bf16[32,128,256]{2,1,0:T(8,128)(2,1)S(1)} %copy-done, f32[1,256]{1,0:T(1,128)S(1)} %bitcast.2, bf16[256,32]{1,0:T(8,128)(2,1)S(1)} %copy.7.wl_ref, bf16[256,32]{1,0:T(8,128)(2,1)S(1)} %copy.8.wr_ref, bf16[1024,128]{1,0:T(8,128)(2,1)S(1)} %copy-done.1, f32[1,128]{1,0:T(1,128)S(1)} %bitcast.3), custom_call_target="tpu_custom_call" | custom-call | flops 11000000512 | bytes 5000000 | tf_op jit(solution)/shard_map/outer_product_mean/pallas_call | solution.py:337
  64.2 1.3 %copy.10 = bf16[64,128,128]{2,1,0:T(8,128)(2,1)} copy(bf16[64,128,128]{2,1,0:T(8,128)(2,1)S(1)} %outer_product_mean.1) | data formatting | bytes 4194304
Async XLA Ops:
  1.7 1.6 %copy-start = (bf16[32,128,256]{2,1,0:T(8,128)(2,1)S(1)}, bf16[32,128,256]{2,1,0:T(8,128)(2,1)}, u32[]{:S(2)}) copy-start(bf16[32,128,256]{2,1,0:T(8,128)(2,1)} %x_ref.1) | copy-start | bytes 6291460
  3.3 0.9 %copy-start.1 = (bf16[1024,128]{1,0:T(8,128)(2,1)S(1)}, bf16[1024,128]{1,0:T(8,128)(2,1)}, u32[]{:S(2)}) copy-start(bf16[1024,128]{1,0:T(8,128)(2,1)} %w_ref.1) | copy-start | bytes 786436
  4.2 0.7 %copy-start.2 = (f32[256]{0:T(256)S(1)}, f32[256]{0:T(256)}, u32[]{:S(2)}) copy-start(f32[256]{0:T(256)} %param.7) | copy-start | bytes 3076
  4.9 0.7 %copy-start.3 = (f32[128]{0:T(128)S(1)}, f32[128]{0:T(128)}, u32[]{:S(2)}) copy-start(f32[128]{0:T(128)} %param.11) | copy-start | bytes 1540

commit v2 on v1

v2 whole, which is shorter than its diff:
```python
import jax
import jax.numpy as jnp
from jax import lax
from jax.experimental import pallas as pl
from jax.experimental.pallas import tpu as pltpu
from jax.sharding import PartitionSpec as P

MESH = pl.DeviceIdType.MESH
BF16, F32 = jnp.bfloat16, jnp.float32
SEQ, RES, CH = 32, 128, 256
HALF, OUTC = 32, 128
ROWS, COLS = 16, 8
SEQ_ALL = SEQ * ROWS
OCT = 8
PIECE = OCT * HALF
NQ = 2
NC = 2
QL = HALF * RES // NQ
QC = HALF * RES // NC
SSTEP = 8
NT = (((1,), (1,)), ((), ()))

R_ROLES = ("sib", "xp", "dn", "up", "oa", "ob", "xdn", "xup", "xoa", "xob")
L_ROLES = ("xp", "dn", "up", "xdn", "xup", "o", "xo")
SUB = 4
EARLY = 2
TRIGGER, TRIGGER_FROM = 'xup', 0
PARTS = (0, 1)
Z_FIRST = (1,)

ORDER = (
    ('e', (
        "r sib 0", "r sib 1", "r xp 0", "r dn 0", "r up 0", "f xp 0", "T", "f dn 0", "f up 0", "r xp 1",
        "f xp 1", "r dn 1", "r up 1", "f dn 1", "f up 1", "l dn 0", "l up 2", "r xdn 0", "r xup 0", "l dn 1",
        "l up 3", "l xp 0", "f xdn 0", "f xup 0", "r oa 0", "r ob 0", "l dn 2", "l up 0", "l xp 2", "f oa 0",
        "f ob 0", "r oa 1", "r ob 1", "l dn 3", "l up 1", "l xp 1", "f oa 1", "f ob 1", "r xoa 0", "r xob 0",
        "l o 0", "l o 2", "l xp 3", "r xdn 1", "f xoa 0", "f xob 0",
    )),
    ('c', (
        (0, 1, 0),
    )),
    ('e', (
        "l o 1", "l o 3", "f xdn 1",
    )),
    ('c', (
        (1, 2, 0),
    )),
    ('e', (
        "l xdn 0", "l xup 0",
    )),
    ('c', (
        (2, 3, 0),
    )),
    ('e', (
        "r xup 1",
    )),
    ('c', (
        (3, 4, 0),
    )),
    ('e', (
        "l xdn 2", "r xoa 1", "l xup 2", "f xup 1",
    )),
    ('c', (
        (4, 5, 0),
    )),
    ('e', (
        "r xob 1", "l xdn 1", "l xup 1", "f xoa 1", "f xob 1",
    )),
    ('c', (
        (0, 1, 1),
    )),
    ('e', (
        "l xdn 3", "l xup 3",
    )),
    ('c', (
        (5, 6, 0),
    )),
    ('e', (
        "l xo 0", "l xo 2",
    )),
    ('c', (
        (6, 7, 0),
    )),
    ('e', (
        "l xo 1",
    )),
    ('c', (
        (1, 3, 1),
    )),
    ('e', (
        "l xo 3",
    )),
    ('c', (
        (7, 8, 0), (3, 8, 1),
    )),
)


def project(x_hbm, x_ref, x_s, scale_ref, wl_ref, wr_ref, z_ref):
    wt = jnp.concatenate([wl_ref[...], wr_ref[...]], axis=0).astype(F32) * scale_ref[...]
    hi = wt.astype(BF16)
    lo = (wt - hi.astype(F32)).astype(BF16)
    colsum = jnp.sum(hi.astype(F32) + lo.astype(F32), axis=1, keepdims=True)
    ones = jnp.ones((16, CH), BF16)
    lhs = jnp.concatenate([hi, lo, ones], axis=0)

    def chunk(k, carry):
        rows = pl.ds(k * SSTEP, SSTEP)
        pltpu.make_async_copy(x_hbm.at[rows], x_ref.at[rows], x_s.at[k]).wait()
        xc = x_ref[rows].reshape(SSTEP * RES, CH)
        p = lax.dot_general(lhs, xc, NT, preferred_element_type=F32)
        xf = xc.astype(F32)
        sq = xf * xf
        sqh = sq.astype(BF16)
        sql = (sq - sqh.astype(F32)).astype(BF16)
        s2 = lax.dot_general(ones, sqh, NT, preferred_element_type=F32) + lax.dot_general(
            ones, sql, NT, preferred_element_type=F32
        )
        mean = p[128:136] * (1.0 / CH)
        mh = mean.astype(BF16).astype(F32)
        ml = mean - mh
        var = (s2[0:8] * (1.0 / CH) - mh * mh) - ml * (2.0 * mh + ml)
        rstd = lax.rsqrt(jnp.maximum(var, 0.0) + 1e-05)
        y = (p[0:64] + p[64:128] - colsum * mean[0:1]) * rstd[0:1]
        for s in range(SSTEP):
            z_ref[k * SSTEP + s] = y[:, s * RES : (s + 1) * RES]
        return carry

    lax.fori_loop(0, SEQ // SSTEP, chunk, 0)


def kernel(
    x_hbm, scale_hbm, wl_hbm, wr_hbm, w_hbm, off_hbm, out_ref,
    x_ref, scale_ref, wl_ref, wr_ref, w_ref, off_ref,
    z_ref, zl_ref, yl_ref, lsend, lt, lf, rf, w2t, wf, ob, acc, outv,
    x_s, p_s, o_s, t_ss, t_rs, l_ss, l_rs, r_ss, r_rs, f_ss, f_rs,
):
    params = ((scale_hbm, scale_ref), (wl_hbm, wl_ref), (wr_hbm, wr_ref), (w_hbm, w_ref), (off_hbm, off_ref))
    params = [pltpu.make_async_copy(a, b, p_s.at[k]) for k, (a, b) in enumerate(params)]
    for d in params[:3]:
        d.start()
    for k in range(SEQ // SSTEP):
        rows = pl.ds(k * SSTEP, SSTEP)
        pltpu.make_async_copy(x_hbm.at[rows], x_ref.at[rows], x_s.at[k]).start()
    for d in params[3:]:
        d.start()

    r, c = lax.axis_index("row"), lax.axis_index("col")
    xl, z, h = r // 8, (r // 2) % 4, r % 2
    xh, y = c // 4, c % 4

    def row_of(xl_, z_, h_):
        return xl_ * 8 + lax.rem(z_ + 4, 4) * 2 + h_

    def col_of(xh_, y_):
        return xh_ * 4 + lax.rem(y_ + 4, 4)

    sib = (row_of(xl, z, 1 - h), c)
    r_dev = {"xp": (row_of(1 - xl, z, h), c), "up": (row_of(xl, z + 1, h), c), "dn": (row_of(xl, z - 1, h), c)}
    l_dev = {"xp": (r, col_of(1 - xh, y)), "up": (r, col_of(xh, y + 1)), "dn": (r, col_of(xh, y - 1))}

    barrier = pltpu.get_barrier_semaphore()
    owner = r // 2
    for dev in (sib, *r_dev.values(), *l_dev.values()):
        pl.semaphore_signal(barrier, inc=1, device_id=dev, device_id_type=MESH)
    for k in range(ROWS):

        @pl.when(jnp.logical_or(k != r, owner != c))
        def _():
            pl.semaphore_signal(barrier, inc=1, device_id=(k, owner), device_id_type=MESH)

    for d in params[:3]:
        d.wait()
    project(x_hbm, x_ref, x_s, scale_ref, wl_ref, wr_ref, z_ref)

    for a in range(HALF):
        yl_ref[a] = z_ref[:, a, :].astype(BF16)
    eye = (
        lax.broadcasted_iota(jnp.int32, (RES, RES), 0) == lax.broadcasted_iota(jnp.int32, (RES, RES), 1)
    ).astype(BF16)
    for t in range(8):
        b = jnp.concatenate([yl_ref[t + 8 * g] for g in range(4)], axis=0)
        zl_ref[:, t, :] = lax.dot_general(eye, b, NT, preferred_element_type=F32)
    lsend[...] = zl_ref[...].reshape(RES * 8, 128).astype(BF16)

    pl.semaphore_wait(barrier, jnp.where(owner == c, 22, 23))

    for k in range(ROWS):
        o = lax.rem(r + k, ROWS)
        to_row, to_col = 2 * c + o // COLS, lax.rem(o, COLS)
        src = lsend.at[pl.ds(pl.multiple_of(o * 64, 64), 64)]
        mine = jnp.logical_and(to_row == r, to_col == c)

        @pl.when(mine)
        def _():
            pltpu.make_async_copy(src, lt.at[r], t_rs.at[r]).start()

        @pl.when(jnp.logical_not(mine))
        def _():
            pltpu.make_async_remote_copy(
                src, lt.at[r], t_ss.at[k], t_rs.at[r], device_id=(to_row, to_col), device_id_type=MESH
            ).start()

    for b in range(HALF):
        rf[pl.ds(pl.multiple_of(r * SEQ, SEQ), SEQ), pl.ds(b * RES, RES)] = z_ref[:, HALF + b, :].astype(BF16)

    def r_ref(q, xl_, z_, h_, half=None):
        rows = row_of(xl_, z_, h_) * SEQ
        n = SEQ
        if half is not None:
            rows, n = rows + half * (SEQ // 2), SEQ // 2
        return rf.at[pl.ds(pl.multiple_of(rows, n), n), pl.ds(q * QL, QL)]

    def r_block(q, role, h_):
        return {
            "own": lambda: r_ref(q, xl, z, h_),
            "xp": lambda: r_ref(q, 1 - xl, z, h_),
            "dn": lambda: r_ref(q, xl, z - 1, h_),
            "up": lambda: r_ref(q, xl, z + 1, h_),
            "oa": lambda: r_ref(q, xl, z + 2, h_, 0),
            "ob": lambda: r_ref(q, xl, z + 2, h_, 1),
            "xdn": lambda: r_ref(q, 1 - xl, z - 1, h_),
            "xup": lambda: r_ref(q, 1 - xl, z + 1, h_),
            "xoa": lambda: r_ref(q, 1 - xl, z + 2, h_, 0),
            "xob": lambda: r_ref(q, 1 - xl, z + 2, h_, 1),
        }[role]()

    def copy(src, sems, at, dev):
        return pltpu.make_async_remote_copy(
            src, src, sems[0].at[at], sems[1].at[at], device_id=dev, device_id_type=MESH
        )

    sends = []

    def r_send(q, role, src, dev):
        d = copy(src, (r_ss, r_rs), (q, R_ROLES.index(role)), dev)
        d.start()
        sends.append(d)

    def f_send(q, role):
        d = copy(r_block(q, role, h), (f_ss, f_rs), (q, R_ROLES.index(role)), sib)
        d.start()
        sends.append(d)

    def r_wait(q, role):
        ref = r_block(q, "own" if role == "sib" else role, 1 - h if role == "sib" else h)
        pltpu.make_async_copy(ref, ref, r_rs.at[q, R_ROLES.index(role)]).wait()

    def f_wait(q, role):
        ref = r_block(q, role, 1 - h)
        pltpu.make_async_copy(ref, ref, f_rs.at[q, R_ROLES.index(role)]).wait()

    def r_own(q):
        own = r_ref(q, xl, z, h)
        r_send(q, "dn", own, r_dev["up"])
        r_send(q, "up", own, r_dev["dn"])
        r_send(q, "xp", own, r_dev["xp"])
        r_send(q, "sib", own, sib)

    def r_event(role, q):
        r_wait(q, role)
        crossed = q not in Z_FIRST
        if role == "dn":
            r_send(q, "oa", r_ref(q, xl, z - 1, h, 0), r_dev["up"])
        elif role == "up":
            r_send(q, "ob", r_ref(q, xl, z + 1, h, 1), r_dev["dn"])
        elif role == "xp" and crossed:
            r_send(q, "xdn", r_block(q, "xp", h), r_dev["up"])
            r_send(q, "xup", r_block(q, "xp", h), r_dev["dn"])
        elif role == "xdn" and crossed:
            r_send(q, "xoa", r_ref(q, 1 - xl, z - 1, h, 0), r_dev["up"])
        elif role == "xup" and crossed:
            r_send(q, "xob", r_ref(q, 1 - xl, z + 1, h, 1), r_dev["dn"])
        if not crossed and role in ("dn", "up", "oa", "ob"):
            r_send(q, "x" + role, r_block(q, role, h), r_dev["xp"])
        if role == TRIGGER and later and q >= TRIGGER_FROM:
            r_own(later.pop(0))
        if role != "sib":
            f_send(q, role)

    l_at = {
        "own": (xh, y), "xp": (1 - xh, y), "dn": (xh, y - 1), "up": (xh, y + 1),
        "xdn": (1 - xh, y - 1), "xup": (1 - xh, y + 1), "o": (xh, y + 2), "xo": (1 - xh, y + 2),
    }
    asc = list(range(SUB))
    desc = asc[SUB // 2 :] + asc[: SUB // 2]

    def l_ref(role, k):
        n = PIECE // SUB
        return lf.at[pl.ds(pl.multiple_of(col_of(*l_at[role]) * PIECE + k * n, n), n)]

    def l_send(role, k, src, dev):
        d = copy(l_ref(src, k), (l_ss, l_rs), (L_ROLES.index(role), k), l_dev[dev])
        d.start()
        sends.append(d)

    def l_wait(role, k):
        ref = l_ref(role, k)
        pltpu.make_async_copy(ref, ref, l_rs.at[L_ROLES.index(role), k]).wait()

    def l_own():
        for k in range(ROWS):
            pltpu.make_async_copy(lt.at[k], lt.at[k], t_rs.at[k]).wait()
        for g in range(4):
            v = jnp.concatenate([lt[4 * g + k] for k in range(4)], axis=1)
            w = jnp.dot(v, perm, preferred_element_type=F32)
            w = jnp.concatenate([w[:, 128 * k : 128 * (k + 1)].reshape(OCT, 8, 128) for k in range(4)], axis=1)
            lf[pl.ds(pl.multiple_of(c * PIECE, PIECE), PIECE), pl.ds(g * 128, 128)] = w.reshape(PIECE, 128).astype(BF16)
        for i in range(SUB):
            l_send("dn", asc[i], "own", "up")
            l_send("up", desc[i], "own", "dn")
            k = (asc, desc)[i % 2][i // 2]
            l_send("xp", k, "own", "xp")

    def l_event(role, k):
        l_wait(role, k)
        if role == "dn" and k < SUB // 2:
            l_send("o", k, "dn", "up")
        elif role == "up" and k >= SUB // 2:
            l_send("o", k, "up", "dn")
        elif role == "xp":
            l_send("xdn", k, "xp", "up")
            l_send("xup", k, "xp", "dn")
        elif role == "xdn" and k < SUB // 2:
            l_send("xo", k, "xdn", "up")
        elif role == "xup" and k >= SUB // 2:
            l_send("xo", k, "xup", "dn")

    def event(name):
        if name == "T":
            l_own()
            return
        kind, role, k = name.split()
        {"r": r_event, "l": l_event, "f": lambda role, q: f_wait(q, role)}[kind](role, int(k))


    def piece_of(k):
        flip = jnp.logical_or(k == 3, k >= 5)
        dy = jnp.where(jnp.logical_or(k == 1, k == 5), 3, jnp.where(jnp.logical_or(k == 2, k == 6), 1, 0))
        dy = jnp.where(jnp.logical_or(k == 4, k == 7), 2, dy)
        return col_of(jnp.where(flip, 1 - xh, xh), y + dy)

    nb = QC // RES

    def outer(k, q, slot):
        lhs = lf[pl.ds(pl.multiple_of(piece_of(k) * PIECE, PIECE), PIECE)]
        o = jnp.dot(lhs, rf[:, pl.ds(pl.multiple_of(q * QC, QC), QC)], preferred_element_type=F32).astype(BF16)
        ob[slot] = jnp.concatenate(
            [
                jnp.concatenate([o[i * HALF : (i + 1) * HALF, b * RES : (b + 1) * RES] for b in range(nb)], axis=0)
                for i in range(OCT)
            ],
            axis=1,
        )

    def final(k, q, slot):
        w = w2t[:, pl.ds(pl.multiple_of(q * nb * HALF, nb * HALF), nb * HALF)]
        acc[k] += jnp.dot(w, ob[slot], preferred_element_type=F32)

    def out_copy(k):
        rows = pl.ds(piece_of(k) * OCT, OCT)
        return pltpu.make_async_copy(outv.at[rows], out_ref.at[rows], o_s.at[k])

    def finish(k):
        m = piece_of(k)
        for i in range(OCT):
            t = acc[k, :, i * RES : (i + 1) * RES].T
            outv[m * OCT + i] = (t * (1.0 / SEQ_ALL) + off).astype(BF16)
        out_copy(k).start()

    def run(first, end, q, before, q_before):
        def step(k, before, done):
            pk, pq, slot = before
            if pk is not None:
                final(pk, pq, slot)
            outer(k, q, 1 - slot)
            if done:
                finish(pk)
            return k, jnp.int32(q), 1 - slot

        before = step(jnp.int32(first), before, q_before == NC - 1)
        if first + 1 < end:
            before = lax.fori_loop(first + 1, end, lambda k, b: step(k, b, q == NC - 1), before)
        return before

    later = list(PARTS[EARLY:])
    for q in PARTS[:EARLY]:
        r_own(q)

    acc[...] = jnp.zeros_like(acc)
    for d in params[3:]:
        d.wait()
    off = off_ref[...]
    i0 = lax.broadcasted_iota(jnp.int32, (512, 512), 0)
    i1 = lax.broadcasted_iota(jnp.int32, (512, 512), 1)
    to = ((i0 // 32) % 4) * 128 + (i0 // 128) * 32 + i0 % 32
    perm = (to == i1).astype(BF16)
    wf[...] = w_ref[...].astype(F32).reshape(HALF, HALF, OUTC)
    for t in range(8):
        blk = jnp.concatenate([wf[:, 4 * t + k, :] for k in range(4)], axis=0)
        w2t[:, pl.ds(t * 128, 128)] = blk.T.astype(BF16)

    before, q_before = (None, jnp.int32(0), jnp.int32(0)), None
    for kind, what in ORDER:
        for x in what:
            if kind == "e":
                event(x)
            else:
                before = run(*x, tuple(jnp.int32(v) if v is not None else v for v in before), q_before)
                q_before = x[2]
    final(*before)
    finish(before[0])
    for k in range(COLS):
        out_copy(k).wait()

    for k in range(ROWS):
        o = lax.rem(r + k, ROWS)
        mine = jnp.logical_and(2 * c + o // COLS == r, lax.rem(o, COLS) == c)

        @pl.when(jnp.logical_not(mine))
        def _():
            src = lsend.at[pl.ds(pl.multiple_of(o * 64, 64), 64)]
            pltpu.make_async_copy(src, src, t_ss.at[k]).wait()

    for d in sends:
        d.wait_send()


def body(x, scale, wl, wr, w, off):
    dma = pltpu.SemaphoreType.DMA
    return pl.pallas_call(
        kernel,
        out_shape=jax.ShapeDtypeStruct((64, RES, OUTC), BF16),
        in_specs=[pl.BlockSpec(memory_space=pltpu.HBM)] * 6,
        out_specs=pl.BlockSpec(memory_space=pltpu.HBM),
        scratch_shapes=[
            pltpu.VMEM((SEQ, RES, CH), BF16),
            pltpu.VMEM((1, CH), F32),
            pltpu.VMEM((HALF, CH), BF16),
            pltpu.VMEM((HALF, CH), BF16),
            pltpu.VMEM((HALF * HALF, OUTC), BF16),
            pltpu.VMEM((1, OUTC), F32),
            pltpu.VMEM((SEQ, 64, RES), F32),
            pltpu.VMEM((RES, 8, 128), F32),
            pltpu.VMEM((HALF, SEQ, RES), BF16),
            pltpu.VMEM((RES * 8, 128), BF16),
            pltpu.VMEM((ROWS, 64, 128), BF16),
            pltpu.VMEM((COLS * PIECE, SEQ_ALL), BF16),
            pltpu.VMEM((SEQ_ALL, HALF * RES), BF16),
            pltpu.VMEM((OUTC, HALF * HALF), BF16),
            pltpu.VMEM((HALF, HALF, OUTC), F32),
            pltpu.VMEM((2, QC // RES * HALF, OCT * RES), BF16),
            pltpu.VMEM((COLS, OUTC, OCT * RES), F32),
            pltpu.VMEM((64, RES, OUTC), BF16),
            dma((SEQ // SSTEP,)), dma((5,)), dma((COLS,)),
            dma((ROWS,)), dma((ROWS,)),
            dma((len(L_ROLES), SUB)), dma((len(L_ROLES), SUB)),
            dma((NQ, len(R_ROLES))), dma((NQ, len(R_ROLES))),
            dma((NQ, len(R_ROLES))), dma((NQ, len(R_ROLES))),
        ],
        compiler_params=pltpu.CompilerParams(
            collective_id=0, has_side_effects=True, vmem_limit_bytes=62 * 2**20
        ),
        cost_estimate=pl.CostEstimate(flops=11 * 10**9, bytes_accessed=5 * 10**6, transcendentals=4096),
        name="outer_product_mean",
    )(x, scale.reshape(1, CH), wl.T, wr.T, w, off.reshape(1, OUTC))


def solution(mesh):
    in_specs = (P("row", "col", None), P(), P(), P(), P(), P())
    return jax.shard_map(body, mesh=mesh, in_specs=in_specs, out_specs=P("row", "col", None), check_vma=False)
```

time: 65.8 us -> 51.6 us (0.78)
  the two profiles are of different devices: /device:TPU:3 before, /device:TPU:0 now
where the time goes in v2:
time: 51.6 us; the launch traced here: 51.4 us
  Pallas kernels  48.2 us (93%)
  local copies, waits for them, and re-layouts  3.16 us (6%)
    pallas_call x1, Pallas kernels, body(): pl.pallas_call(kernel, out_shape=jax.ShapeDtypeStruct((64, RES, OUTC), BF...  48.2 us
    unnamed x1, local copies, waits for them, and re-layouts  3.16 us

profile of v2, /device:TPU:0, one launch (start us, length us, event | category | flops | bytes accessed | tf_op | source)
XLA Modules:
  0.0 51.4 jit_solution(16976938260717483628)
XLA Ops:
  0.0 48.2 %outer_product_mean.1 = bf16[64,128,128]{2,1,0:T(8,128)(2,1)} custom-call(bf16[32,128,256]{2,1,0:T(8,128)(2,1)} %x_hbm.1, f32[1,256]{1,0:T(1,128)} %bitcast.6, bf16[32,256]{1,0:T(8,128)(2,1)} %bitcast.4, bf16[32,256]{1,0:T(8,128)(2,1)} %bitcast.5, bf16[1024,128]{1,0:T(8,128)(2,1)} %w_hbm.1, f32[1,128]{1,0:T(1,128)} %bitcast.7), custom_call_target="tpu_custom_call" | custom-call | flops 11000000512 | bytes 5000000 | tf_op jit(solution)/shard_map/outer_product_mean/pallas_call | solution.py:431
  48.3 3.2 %copy.8 = bf16[64,128,128]{2,1,0:T(8,128)(2,1)} copy(bf16[64,128,128]{2,1,0:T(8,128)(2,1)} %outer_product_mean.1) | data formatting | bytes 4194304

commit v3 on v2

--- a/solution.py
+++ b/solution.py
@@ -13,85 +13,82 @@
 SEQ_ALL = SEQ * ROWS
 OCT = 8
 PIECE = OCT * HALF
-NQ = 2
-NC = 2
+NQ = 4
+NC = 4
 QL = HALF * RES // NQ
 QC = HALF * RES // NC
 SSTEP = 8
 NT = (((1,), (1,)), ((), ()))
 
 R_ROLES = ("sib", "xp", "dn", "up", "oa", "ob", "xdn", "xup", "xoa", "xob")
-L_ROLES = ("xp", "dn", "up", "xdn", "xup", "o", "xo")
-SUB = 4
+PIECES = ("own", "dn", "up", "xp", "o", "xdn", "xup", "xo")
+PAIR = 2
+SUB = 2
 EARLY = 2
-TRIGGER, TRIGGER_FROM = 'xup', 0
-PARTS = (0, 1)
-Z_FIRST = (1,)
+TRIGGER, TRIGGER_FROM = 'dn', 0
+PARTS = (0, 1, 2, 3)
+Z_FIRST = (3,)
 
 ORDER = (
     ('e', (
-        "r sib 0", "r sib 1", "r xp 0", "r dn 0", "r up 0", "f xp 0", "T", "f dn 0", "f up 0", "r xp 1",
-        "f xp 1", "r dn 1", "r up 1", "f dn 1", "f up 1", "l dn 0", "l up 2", "r xdn 0", "r xup 0", "l dn 1",
-        "l up 3", "l xp 0", "f xdn 0", "f xup 0", "r oa 0", "r ob 0", "l dn 2", "l up 0", "l xp 2", "f oa 0",
-        "f ob 0", "r oa 1", "r ob 1", "l dn 3", "l up 1", "l xp 1", "f oa 1", "f ob 1", "r xoa 0", "r xob 0",
-        "l o 0", "l o 2", "l xp 3", "r xdn 1", "f xoa 0", "f xob 0",
+        "r sib 0", "r sib 1", "r xp 0", "r dn 0", "r up 0", "r xp 1", "r dn 1", "r up 1", "f xp 0", "T",
+        "r sib 2", "f dn 0", "f up 0", "f xp 1", "r xdn 0", "r xup 0", "r xp 2", "r sib 3", "f dn 1", "r oa 0",
+        "f up 1", "r up 2", "r xp 3", "f xdn 0", "r dn 2", "r ob 0", "f xup 0", "f xp 2", "f oa 0", "f up 2",
+        "r xdn 1", "r xup 1", "f xp 3", "f dn 2", "f ob 0", "r oa 1", "l dn 0", "l up 1", "r up 3", "f xdn 1",
+        "r dn 3", "r ob 1", "f xup 1", "f oa 1", "l xp 0", "r xoa 0", "r xob 0", "f up 3", "l dn 1", "l up 0",
+        "f dn 3", "f ob 1", "r xdn 2", "r xup 2", "r xup 3", "f xoa 0", "f xob 0",
     )),
     ('c', (
         (0, 1, 0),
     )),
     ('e', (
-        "l o 1", "l o 3", "f xdn 1",
+        "r oa 2", "r ob 2", "l xp 1", "r xoa 1", "r xob 1",
     )),
     ('c', (
         (1, 2, 0),
     )),
     ('e', (
-        "l xdn 0", "l xup 0",
+        "r xdn 3", "f xdn 2", "r oa 3", "r ob 3", "l o 0", "l o 1", "f xup 2", "f xup 3", "r xoa 2", "r xob 2",
+        "f oa 2", "f ob 2", "f xoa 1", "f xob 1",
+    )),
+    ('c', (
+        (0, 2, 1),
+    )),
+    ('e', (
+        "f xdn 3", "f oa 3", "f ob 3", "f xoa 2", "f xob 2", "l xdn 0", "l xup 0", "r xoa 3",
+    )),
+    ('c', (
+        (0, 1, 2),
+    )),
+    ('e', (
+        "r xob 3",
+    )),
+    ('c', (
+        (1, 2, 2),
+    )),
+    ('e', (
+        "f xoa 3", "l xdn 1", "l xup 1",
     )),
     ('c', (
         (2, 3, 0),
     )),
     ('e', (
-        "r xup 1",
-    )),
-    ('c', (
-        (3, 4, 0),
-    )),
-    ('e', (
-        "l xdn 2", "r xoa 1", "l xup 2", "f xup 1",
-    )),
-    ('c', (
-        (4, 5, 0),
-    )),
-    ('e', (
-        "r xob 1", "l xdn 1", "l xup 1", "f xoa 1", "f xob 1",
-    )),
-    ('c', (
-        (0, 1, 1),
-    )),
-    ('e', (
-        "l xdn 3", "l xup 3",
-    )),
-    ('c', (
-        (5, 6, 0),
-    )),
-    ('e', (
-        "l xo 0", "l xo 2",
-    )),
-    ('c', (
-        (6, 7, 0),
+        "f xob 3",
+    )),
+    ('c', (
+        (2, 3, 1), (2, 3, 2), (0, 1, 3),
+    )),
+    ('e', (
+        "l xo 0",
+    )),
+    ('c', (
+        (1, 3, 3),
     )),
     ('e', (
         "l xo 1",
     )),
     ('c', (
-        (1, 3, 1),
-    )),
-    ('e', (
-        "l xo 3",
-    )),
-    ('c', (
-        (7, 8, 0), (3, 8, 1),
+        (3, 4, 0), (3, 4, 1), (3, 4, 2), (3, 4, 3),
     )),
 )
 
@@ -278,25 +275,24 @@
         if role != "sib":
             f_send(q, role)
 
-    l_at = {
-        "own": (xh, y), "xp": (1 - xh, y), "dn": (xh, y - 1), "up": (xh, y + 1),
-        "xdn": (1 - xh, y - 1), "xup": (1 - xh, y + 1), "o": (xh, y + 2), "xo": (1 - xh, y + 2),
-    }
     asc = list(range(SUB))
     desc = asc[SUB // 2 :] + asc[: SUB // 2]
 
     def l_ref(role, k):
         n = PIECE // SUB
-        return lf.at[pl.ds(pl.multiple_of(col_of(*l_at[role]) * PIECE + k * n, n), n)]
+        return lf.at[pl.ds(PIECES.index(role) * PIECE + k * n, n)]
 
     def l_send(role, k, src, dev):
-        d = copy(l_ref(src, k), (l_ss, l_rs), (L_ROLES.index(role), k), l_dev[dev])
+        at = (PIECES.index(role), k)
+        d = pltpu.make_async_remote_copy(
+            l_ref(src, k), l_ref(role, k), l_ss.at[at], l_rs.at[at], device_id=l_dev[dev], device_id_type=MESH
+        )
         d.start()
         sends.append(d)
 
     def l_wait(role, k):
         ref = l_ref(role, k)
-        pltpu.make_async_copy(ref, ref, l_rs.at[L_ROLES.index(role), k]).wait()
+        pltpu.make_async_copy(ref, ref, l_rs.at[PIECES.index(role), k]).wait()
 
     def l_own():
         for k in range(ROWS):
@@ -305,7 +301,7 @@
             v = jnp.concatenate([lt[4 * g + k] for k in range(4)], axis=1)
             w = jnp.dot(v, perm, preferred_element_type=F32)
             w = jnp.concatenate([w[:, 128 * k : 128 * (k + 1)].reshape(OCT, 8, 128) for k in range(4)], axis=1)
-            lf[pl.ds(pl.multiple_of(c * PIECE, PIECE), PIECE), pl.ds(g * 128, 128)] = w.reshape(PIECE, 128).astype(BF16)
+            lf[pl.ds(0, PIECE), pl.ds(g * 128, 128)] = w.reshape(PIECE, 128).astype(BF16)
         for i in range(SUB):
             l_send("dn", asc[i], "own", "up")
             l_send("up", desc[i], "own", "dn")
@@ -342,31 +338,35 @@
 
     nb = QC // RES
 
-    def outer(k, q, slot):
-        lhs = lf[pl.ds(pl.multiple_of(piece_of(k) * PIECE, PIECE), PIECE)]
+    rows = PAIR * OCT
+
+    def outer(p, q, slot):
+        lhs = lf[pl.ds(pl.multiple_of(p * PAIR * PIECE, PIECE), PAIR * PIECE)]
         o = jnp.dot(lhs, rf[:, pl.ds(pl.multiple_of(q * QC, QC), QC)], preferred_element_type=F32).astype(BF16)
         ob[slot] = jnp.concatenate(
             [
                 jnp.concatenate([o[i * HALF : (i + 1) * HALF, b * RES : (b + 1) * RES] for b in range(nb)], axis=0)
-                for i in range(OCT)
+                for i in range(rows)
             ],
             axis=1,
         )
 
-    def final(k, q, slot):
+    def final(p, q, slot):
         w = w2t[:, pl.ds(pl.multiple_of(q * nb * HALF, nb * HALF), nb * HALF)]
-        acc[k] += jnp.dot(w, ob[slot], preferred_element_type=F32)
+        acc[p] += jnp.dot(w, ob[slot], preferred_element_type=F32)
 
     def out_copy(k):
         rows = pl.ds(piece_of(k) * OCT, OCT)
         return pltpu.make_async_copy(outv.at[rows], out_ref.at[rows], o_s.at[k])
 
-    def finish(k):
-        m = piece_of(k)
-        for i in range(OCT):
-            t = acc[k, :, i * RES : (i + 1) * RES].T
-            outv[m * OCT + i] = (t * (1.0 / SEQ_ALL) + off).astype(BF16)
-        out_copy(k).start()
+    def finish(p):
+        for k in range(PAIR):
+            m = piece_of(p * PAIR + k)
+            for i in range(OCT):
+                at = (k * OCT + i) * RES
+                t = acc[p, :, at : at + RES].T
+                outv[m * OCT + i] = (t * (1.0 / SEQ_ALL) + off).astype(BF16)
+            out_copy(p * PAIR + k).start()
 
     def run(first, end, q, before, q_before):
         def step(k, before, done):
@@ -426,9 +426,22 @@
         d.wait_send()
 
 
+def place(src, dst, held, sems):
+    parts = [pl.ds(k * OCT, OCT) for k in range(COLS)]
+    ins = [pltpu.make_async_copy(src.at[p], held.at[p], sems.at[0, k]) for k, p in enumerate(parts)]
+    outs = [pltpu.make_async_copy(held.at[p], dst.at[p], sems.at[1, k]) for k, p in enumerate(parts)]
+    for d in ins:
+        d.start()
+    for d, e in zip(ins, outs):
+        d.wait()
+        e.start()
+    for e in outs:
+        e.wait()
+
+
 def body(x, scale, wl, wr, w, off):
     dma = pltpu.SemaphoreType.DMA
-    return pl.pallas_call(
+    out = pl.pallas_call(
         kernel,
         out_shape=jax.ShapeDtypeStruct((64, RES, OUTC), BF16),
         in_specs=[pl.BlockSpec(memory_space=pltpu.HBM)] * 6,
@@ -449,12 +462,12 @@
             pltpu.VMEM((SEQ_ALL, HALF * RES), BF16),
             pltpu.VMEM((OUTC, HALF * HALF), BF16),
             pltpu.VMEM((HALF, HALF, OUTC), F32),
-            pltpu.VMEM((2, QC // RES * HALF, OCT * RES), BF16),
-            pltpu.VMEM((COLS, OUTC, OCT * RES), F32),
+            pltpu.VMEM((2, QC // RES * HALF, PAIR * OCT * RES), BF16),
+            pltpu.VMEM((COLS // PAIR, OUTC, PAIR * OCT * RES), F32),
             pltpu.VMEM((64, RES, OUTC), BF16),
             dma((SEQ // SSTEP,)), dma((5,)), dma((COLS,)),
             dma((ROWS,)), dma((ROWS,)),
-            dma((len(L_ROLES), SUB)), dma((len(L_ROLES), SUB)),
+            dma((COLS, SUB)), dma((COLS, SUB)),
             dma((NQ, len(R_ROLES))), dma((NQ, len(R_ROLES))),
             dma((NQ, len(R_ROLES))), dma((NQ, len(R_ROLES))),
         ],
@@ -464,6 +477,15 @@
         cost_estimate=pl.CostEstimate(flops=11 * 10**9, bytes_accessed=5 * 10**6, transcendentals=4096),
         name="outer_product_mean",
     )(x, scale.reshape(1, CH), wl.T, wr.T, w, off.reshape(1, OUTC))
+    return pl.pallas_call(
+        place,
+        out_shape=jax.ShapeDtypeStruct(out.shape, out.dtype),
+        in_specs=[pl.BlockSpec(memory_space=pltpu.HBM)],
+        out_specs=pl.BlockSpec(memory_space=pltpu.HBM),
+        scratch_shapes=[pltpu.VMEM((64, RES, OUTC), BF16), dma((2, COLS))],
+        compiler_params=pltpu.CompilerParams(vmem_limit_bytes=62 * 2**20),
+        name="place",
+    )(out)
 
 
 def solution(mesh):

time: 51.6 us -> 48.5 us (0.940)
  local copies, waits for them, and re-layouts: 3.16 us -> 0 us
    unnamed x1 -> x0, local copies, waits for them, and re-layouts: 3.16 us -> none
    pallas_call x0 -> x1, Pallas kernels: none -> 2.4 us  [body(): pl.pallas_call(place, out_shape=jax.ShapeDtypeStruct(out.shape, out.dtype...]
    pallas_call x1, Pallas kernels: 48.2 us -> 45.9 us  [body(): pl.pallas_call(kernel, out_shape=jax.ShapeDtypeStruct((64, RES, OUTC), BF...]
where the time goes in v3:
time: 48.5 us; the launch traced here: 48.3 us
  Pallas kernels  48.3 us (100%)
    pallas_call x1, Pallas kernels, body(): pl.pallas_call(kernel, out_shape=jax.ShapeDtypeStruct((64, RES, OUTC), BF...  45.9 us
    pallas_call x1, Pallas kernels, body(): pl.pallas_call(place, out_shape=jax.ShapeDtypeStruct(out.shape, out.dtype...  2.4 us

profile of v3, /device:TPU:0, one launch (start us, length us, event | category | flops | bytes accessed | tf_op | source)
XLA Modules:
  0.0 48.3 jit_solution(8757117576685241026)
XLA Ops:
  0.0 45.9 %outer_product_mean.1.src = bf16[64,128,128]{2,1,0:T(8,128)(2,1)} custom-call(bf16[32,128,256]{2,1,0:T(8,128)(2,1)} %x_hbm.1, f32[1,256]{1,0:T(1,128)} %bitcast.6, bf16[32,256]{1,0:T(8,128)(2,1)} %bitcast.4, bf16[32,256]{1,0:T(8,128)(2,1)} %bitcast.5, bf16[1024,128]{1,0:T(8,128)(2,1)} %w_hbm.1, f32[1,128]{1,0:T(1,128)} %bitcast.7), custom_call_target="tpu_custom_call" | custom-call | flops 11000000512 | bytes 5000000 | tf_op jit(solution)/shard_map/outer_product_mean/pallas_call | solution.py:444
  45.9 2.4 %place.1 = bf16[64,128,128]{2,1,0:T(8,128)(2,1)} custom-call(bf16[64,128,128]{2,1,0:T(8,128)(2,1)} %outer_product_mean.1.src), custom_call_target="tpu_custom_call" | custom-call | tf_op jit(solution)/shard_map/place/pallas_call | solution.py:480

commit v4 on v3

--- a/solution.py
+++ b/solution.py
@@ -24,65 +24,72 @@
 PIECES = ("own", "dn", "up", "xp", "o", "xdn", "xup", "xo")
 PAIR = 2
 SUB = 2
-EARLY = 2
+EARLY = 3
 TRIGGER, TRIGGER_FROM = 'dn', 0
 PARTS = (0, 1, 2, 3)
 Z_FIRST = (3,)
 
 ORDER = (
     ('e', (
-        "r sib 0", "r sib 1", "r xp 0", "r dn 0", "r up 0", "r xp 1", "r dn 1", "r up 1", "f xp 0", "T",
-        "r sib 2", "f dn 0", "f up 0", "f xp 1", "r xdn 0", "r xup 0", "r xp 2", "r sib 3", "f dn 1", "r oa 0",
-        "f up 1", "r up 2", "r xp 3", "f xdn 0", "r dn 2", "r ob 0", "f xup 0", "f xp 2", "f oa 0", "f up 2",
-        "r xdn 1", "r xup 1", "f xp 3", "f dn 2", "f ob 0", "r oa 1", "l dn 0", "l up 1", "r up 3", "f xdn 1",
-        "r dn 3", "r ob 1", "f xup 1", "f oa 1", "l xp 0", "r xoa 0", "r xob 0", "f up 3", "l dn 1", "l up 0",
-        "f dn 3", "f ob 1", "r xdn 2", "r xup 2", "r xup 3", "f xoa 0", "f xob 0",
+        "r sib 0", "r sib 1", "r sib 2", "r xp 0", "r dn 0", "r up 0", "r xp 1", "r dn 1", "r up 1", "f xp 0",
+        "T", "r xp 2", "r sib 3", "f dn 0", "f up 0", "f xp 1", "r dn 2", "r up 2", "r xp 3", "f dn 1",
+        "f up 1", "r xdn 0", "r xup 0", "f xp 2", "f dn 2", "r oa 0", "f up 2", "f xp 3", "r up 3", "f xdn 0",
+        "r dn 3", "r ob 0", "f xup 0", "f oa 0", "l dn 0", "l up 0", "f up 3", "r xdn 1", "r xup 1", "f dn 3",
+        "f ob 0", "r oa 1", "r ob 1", "l xp 0", "f xdn 1", "r xdn 2", "r xup 2", "f xup 1", "l dn 1", "l up 1",
+        "f oa 1", "f ob 1", "r oa 2", "r ob 2", "r xup 3", "r xoa 0", "r xob 0", "l xp 1", "f xdn 2", "r oa 3",
+        "r ob 3", "r xdn 3", "f xup 2", "f oa 2", "f ob 2", "r xoa 1", "r xob 1", "f xup 3", "l o 0",
+        "f xoa 0", "f xob 0",
     )),
     ('c', (
         (0, 1, 0),
     )),
     ('e', (
-        "r oa 2", "r ob 2", "l xp 1", "r xoa 1", "r xob 1",
+        "r xoa 2", "r xob 2", "l xup 0", "f oa 3", "f ob 3", "f xdn 3",
     )),
     ('c', (
         (1, 2, 0),
     )),
     ('e', (
-        "r xdn 3", "f xdn 2", "r oa 3", "r ob 3", "l o 0", "l o 1", "f xup 2", "f xup 3", "r xoa 2", "r xob 2",
-        "f oa 2", "f ob 2", "f xoa 1", "f xob 1",
-    )),
-    ('c', (
-        (0, 2, 1),
-    )),
-    ('e', (
-        "f xdn 3", "f oa 3", "f ob 3", "f xoa 2", "f xob 2", "l xdn 0", "l xup 0", "r xoa 3",
+        "f xoa 1", "r xoa 3", "f xob 1",
+    )),
+    ('c', (
+        (0, 1, 1),
+    )),
+    ('e', (
+        "r xob 3", "l xdn 0", "f xoa 2", "f xob 2",
+    )),
+    ('c', (
+        (1, 2, 1),
+    )),
+    ('e', (
+        "l o 1",
     )),
     ('c', (
         (0, 1, 2),
     )),
     ('e', (
-        "r xob 3",
+        "f xoa 3",
     )),
     ('c', (
         (1, 2, 2),
     )),
     ('e', (
-        "f xoa 3", "l xdn 1", "l xup 1",
+        "f xob 3", "l xdn 1",
     )),
     ('c', (
         (2, 3, 0),
     )),
     ('e', (
-        "f xob 3",
-    )),
-    ('c', (
-        (2, 3, 1), (2, 3, 2), (0, 1, 3),
+        "l xup 1",
+    )),
+    ('c', (
+        (2, 3, 1),
     )),
     ('e', (
         "l xo 0",
     )),
     ('c', (
-        (1, 3, 3),
+        (2, 3, 2), (0, 3, 3),
     )),
     ('e', (
         "l xo 1",
@@ -183,9 +190,9 @@
     pl.semaphore_wait(barrier, jnp.where(owner == c, 22, 23))
 
     for k in range(ROWS):
-        o = lax.rem(r + k, ROWS)
-        to_row, to_col = 2 * c + o // COLS, lax.rem(o, COLS)
-        src = lsend.at[pl.ds(pl.multiple_of(o * 64, 64), 64)]
+        o = k
+        to_row, to_col = 2 * c + o // COLS, o % COLS
+        src = lsend.at[pl.ds(o * 64, 64)]
         mine = jnp.logical_and(to_row == r, to_col == c)
 
         @pl.when(mine)
@@ -249,9 +256,9 @@
 
     def r_own(q):
         own = r_ref(q, xl, z, h)
+        r_send(q, "xp", own, r_dev["xp"])
         r_send(q, "dn", own, r_dev["up"])
         r_send(q, "up", own, r_dev["dn"])
-        r_send(q, "xp", own, r_dev["xp"])
         r_send(q, "sib", own, sib)
 
     def r_event(role, q):
@@ -297,16 +304,15 @@
     def l_own():
         for k in range(ROWS):
             pltpu.make_async_copy(lt.at[k], lt.at[k], t_rs.at[k]).wait()
+        v = jnp.concatenate([jnp.concatenate([lt[4 * g + k] for k in range(4)], axis=1) for g in range(4)], axis=0)
+        w = jnp.dot(v, perm, preferred_element_type=F32)
         for g in range(4):
-            v = jnp.concatenate([lt[4 * g + k] for k in range(4)], axis=1)
-            w = jnp.dot(v, perm, preferred_element_type=F32)
-            w = jnp.concatenate([w[:, 128 * k : 128 * (k + 1)].reshape(OCT, 8, 128) for k in range(4)], axis=1)
-            lf[pl.ds(0, PIECE), pl.ds(g * 128, 128)] = w.reshape(PIECE, 128).astype(BF16)
+            u = [w[64 * g : 64 * (g + 1), 128 * k : 128 * (k + 1)].reshape(OCT, 8, 128) for k in range(4)]
+            lf[pl.ds(0, PIECE), pl.ds(g * 128, 128)] = jnp.concatenate(u, axis=1).reshape(PIECE, 128).astype(BF16)
         for i in range(SUB):
+            l_send("xp", (asc, desc)[i % 2][i // 2], "own", "xp")
             l_send("dn", asc[i], "own", "up")
             l_send("up", desc[i], "own", "dn")
-            k = (asc, desc)[i % 2][i // 2]
-            l_send("xp", k, "own", "xp")
 
     def l_event(role, k):
         l_wait(role, k)
@@ -317,10 +323,8 @@
         elif role == "xp":
             l_send("xdn", k, "xp", "up")
             l_send("xup", k, "xp", "dn")
-        elif role == "xdn" and k < SUB // 2:
-            l_send("xo", k, "xdn", "up")
-        elif role == "xup" and k >= SUB // 2:
-            l_send("xo", k, "xup", "dn")
+        elif role == "o":
+            l_send("xo", k, "o", "xp")
 
     def event(name):
         if name == "T":
@@ -414,12 +418,12 @@
         out_copy(k).wait()
 
     for k in range(ROWS):
-        o = lax.rem(r + k, ROWS)
-        mine = jnp.logical_and(2 * c + o // COLS == r, lax.rem(o, COLS) == c)
+        o = k
+        mine = jnp.logical_and(2 * c + o // COLS == r, o % COLS == c)
 
         @pl.when(jnp.logical_not(mine))
         def _():
-            src = lsend.at[pl.ds(pl.multiple_of(o * 64, 64), 64)]
+            src = lsend.at[pl.ds(o * 64, 64)]
             pltpu.make_async_copy(src, src, t_ss.at[k]).wait()
 
     for d in sends:

time: 48.5 us -> 48.2 us (level)
  Pallas kernels: 48.3 us -> 47.5 us
    pallas_call x1, Pallas kernels: 45.9 us -> 45.1 us  [body(): pl.pallas_call(kernel, out_shape=jax.ShapeDtypeStruct((64, RES, OUTC), BF...]
where the time goes in v4:
time: 48.2 us; the launch traced here: 47.5 us
  Pallas kernels  47.5 us (99%)
    pallas_call x1, Pallas kernels, body(): pl.pallas_call(kernel, out_shape=jax.ShapeDtypeStruct((64, RES, OUTC), BF...  45.1 us
    pallas_call x1, Pallas kernels, body(): pl.pallas_call(place, out_shape=jax.ShapeDtypeStruct(out.shape, out.dtype...  2.4 us

profile of v4, /device:TPU:0, one launch (start us, length us, event | category | flops | bytes accessed | tf_op | source)
XLA Modules:
  0.0 47.5 jit_solution(7882385408186477192)
XLA Ops:
  0.0 45.1 %outer_product_mean.1.src = bf16[64,128,128]{2,1,0:T(8,128)(2,1)} custom-call(bf16[32,128,256]{2,1,0:T(8,128)(2,1)} %x_hbm.1, f32[1,256]{1,0:T(1,128)} %bitcast.6, bf16[32,256]{1,0:T(8,128)(2,1)} %bitcast.4, bf16[32,256]{1,0:T(8,128)(2,1)} %bitcast.5, bf16[1024,128]{1,0:T(8,128)(2,1)} %w_hbm.1, f32[1,128]{1,0:T(1,128)} %bitcast.7), custom_call_target="tpu_custom_call" | custom-call | flops 11000000512 | bytes 5000000 | tf_op jit(solution)/shard_map/outer_product_mean/pallas_call | solution.py:448
  45.1 2.4 %place.1 = bf16[64,128,128]{2,1,0:T(8,128)(2,1)} custom-call(bf16[64,128,128]{2,1,0:T(8,128)(2,1)} %outer_product_mean.1.src), custom_call_target="tpu_custom_call" | custom-call | tf_op jit(solution)/shard_map/place/pallas_call | solution.py:484

commit v5 on v4

--- a/solution.py
+++ b/solution.py
@@ -130,7 +130,7 @@
             z_ref[k * SSTEP + s] = y[:, s * RES : (s + 1) * RES]
         return carry
 
-    lax.fori_loop(0, SEQ // SSTEP, chunk, 0)
+    lax.fori_loop(0, SEQ // SSTEP, chunk, 0, unroll=True)
 
 
 def kernel(

time: 48.2 us -> 48.3 us (level)
  no operation moved by 1% of the time
where the time goes in v5:
time: 48.3 us; the launch traced here: 47.7 us
  Pallas kernels  47.6 us (99%)
    pallas_call x1, Pallas kernels, body(): pl.pallas_call(kernel, out_shape=jax.ShapeDtypeStruct((64, RES, OUTC), BF...  45.2 us
    pallas_call x1, Pallas kernels, body(): pl.pallas_call(place, out_shape=jax.ShapeDtypeStruct(out.shape, out.dtype...  2.4 us

profile of v5, /device:TPU:0, one launch (start us, length us, event | category | flops | bytes accessed | tf_op | source)
XLA Modules:
  0.0 47.7 jit_solution(3730783321387549063)
XLA Ops:
  0.0 45.2 %outer_product_mean.1.src = bf16[64,128,128]{2,1,0:T(8,128)(2,1)} custom-call(bf16[32,128,256]{2,1,0:T(8,128)(2,1)} %x_hbm.1, f32[1,256]{1,0:T(1,128)} %bitcast.6, bf16[32,256]{1,0:T(8,128)(2,1)} %bitcast.4, bf16[32,256]{1,0:T(8,128)(2,1)} %bitcast.5, bf16[1024,128]{1,0:T(8,128)(2,1)} %w_hbm.1, f32[1,128]{1,0:T(1,128)} %bitcast.7), custom_call_target="tpu_custom_call" | custom-call | flops 11000000512 | bytes 5000000 | tf_op jit(solution)/shard_map/outer_product_mean/pallas_call | solution.py:448
  45.2 2.4 %place.1 = bf16[64,128,128]{2,1,0:T(8,128)(2,1)} custom-call(bf16[64,128,128]{2,1,0:T(8,128)(2,1)} %outer_product_mean.1.src), custom_call_target="tpu_custom_call" | custom-call | tf_op jit(solution)/shard_map/place/pallas_call | solution.py:484
